TPU v7x, 128 devices: a whole 4x4x4 slice. The times are simulated.
128 devices in a mesh: box: 16 (over z, x), dir: 8 (over y, core).
Axes of the slice: x: 4, y: 4, z: 4, core: 2. Of those that a mesh axis runs over, the one named last changes fastest.
Arguments:
- currents: bfloat16 [2048, 128, 128], P(('box', 'dir')), may hold values from -6 to 6
- near_blocks: bfloat16 [2048, 8, 128, 256], P(('box', 'dir')), may hold values from -0.375 to 0.375
- near_list: int32 [2048, 8], P(('box', 'dir')), may hold values from 0 to 2047, as said below
- near_count: int32 [2048], P(('box', 'dir')), may hold values from 2 to 8, as said below
- radiation: bfloat16 [1024, 256], replicated, may hold values from -0.375 to 0.375
- child_angle: float32 [2048, 1024], P(('box', 'dir')), may hold values from -3.140625 to 3.140625
- translation: float32 [316, 2, 1024], replicated, may hold values from -0.61237246 to 0.61237246
- inter_src: int32 [128, 6], replicated, may hold values from 0 to 127, as said below
- inter_off: int32 [128, 6], replicated, may hold values from 0 to 315
- inter_count: int32 [128], replicated, may hold values from 2 to 6, as said below
Outputs:
- field: bfloat16 [2048, 128, 128], P(('box', 'dir'))
Inputs may be any that keep to these rules, and one draw needn't show every extreme that they name: `near_list`: entry k of leaf box b names a box at most 8 away from b; entry 0 is b itself and entry 1 lies exactly 8 away. Slots at or beyond near_count[b] of near_list and near_blocks are padding and are not used. `inter_src`: each row names 6 different upper-level boxes, none equal to the row's own. Only the first inter_count[p] slots of row p of inter_src and inter_off are used.
All inputs are finite; a program needn't handle non-finite values.
Results may differ from a plain program's by a relative error of at most 0.006.
Values may be sent and summed in bfloat16 or wider, within the bound.
A program may use at most 128 MiB of HBM per device.

v0:
```python
import jax
import jax.numpy as jnp
from jax import lax
from jax.sharding import PartitionSpec as P

CHILD = 16


def padded(cells, sides, width):
    for axis, dim in sides:
        count = lax.axis_size(axis)
        ends = count - 1
        head = lax.slice_in_dim(cells, 0, width, axis=dim)
        tail = lax.slice_in_dim(cells, cells.shape[dim] - width, cells.shape[dim], axis=dim)
        cells = jnp.concatenate(
            [
                lax.ppermute(tail, axis, [(i, (i + 1) % count) for i in range(ends)]),
                cells,
                lax.ppermute(head, axis, [((i + 1) % count, i) for i in range(ends)]),
            ],
            axis=dim,
        )
    return cells


def turned(values):
    half_width = values.shape[-1] // 2
    return jnp.concatenate([-values[..., half_width:], values[..., :half_width]], axis=-1)


def coefficients(translation, src_rows, off_rows, count_rows, source_width, dir_start, dir_width):
    operators = jnp.take(translation, off_rows, axis=0)
    operators = lax.dynamic_slice_in_dim(operators, dir_start, dir_width, 3)
    slot_ids = jnp.arange(src_rows.shape[1], dtype=jnp.int32)
    live_slot = slot_ids[None, :] < count_rows[:, None]
    source_ids = jnp.arange(source_width, dtype=jnp.int32)
    selector = ((src_rows[:, :, None] == source_ids[None, None, :]) & live_slot[:, :, None]).astype(
        jnp.float32
    )
    return jnp.einsum("tks,tkcq->tscq", selector, operators, precision=lax.Precision.HIGHEST)


def apply_coef(coef, pieces):
    highest = lax.Precision.HIGHEST
    pieces_full = pieces.astype(jnp.float32)
    half_width = pieces.shape[-1] // 2
    real_part = pieces_full[..., :half_width]
    imag_part = pieces_full[..., half_width:]
    real_op = coef[:, :, 0, :]
    imag_op = coef[:, :, 1, :]
    real_out = jnp.einsum("tsq,sqr->tqr", real_op, real_part, precision=highest) - jnp.einsum(
        "tsq,sqr->tqr", imag_op, imag_part, precision=highest
    )
    imag_out = jnp.einsum("tsq,sqr->tqr", real_op, imag_part, precision=highest) + jnp.einsum(
        "tsq,sqr->tqr", imag_op, real_part, precision=highest
    )
    return jnp.concatenate([real_out, imag_out], axis=-1)


def local(
    currents,
    near_blocks,
    near_list,
    near_count,
    radiation,
    child_angle,
    translation,
    inter_src,
    inter_off,
    inter_count,
):
    boxes_dev = currents.shape[0]
    slot_count = near_list.shape[1]
    unknowns = currents.shape[1]
    rhs_width = currents.shape[2] // 2
    directions = radiation.shape[0]
    rim_width = boxes_dev // 2
    dir_count = lax.axis_size("dir")
    dir_rank = lax.axis_index("dir")
    box_rank = lax.axis_index("box")
    first_box = (box_rank * dir_count + dir_rank) * boxes_dev
    parents_dev = boxes_dev // CHILD
    group_size = parents_dev * dir_count
    group_first = box_rank * group_size
    dir_width = directions // dir_count
    dir_start = dir_rank * dir_width
    extended = padded(currents, ((("box", "dir"), 0),), rim_width)
    slot_ids = jnp.arange(slot_count, dtype=jnp.int32)
    live_slot = slot_ids[None, :] < near_count[:, None]
    local_ids = near_list - (first_box - rim_width)
    local_ids = jnp.where(live_slot, local_ids, extended.shape[0])
    neighbours = jnp.take(extended, local_ids, axis=0, mode="fill", fill_value=0)
    split_blocks = near_blocks.reshape(boxes_dev, slot_count, unknowns, 2, unknowns)
    halves = jnp.einsum(
        "bkpcj,bkjr->bcpr", split_blocks, neighbours, preferred_element_type=jnp.float32
    )
    near_part = halves[:, 0] + turned(halves[:, 1])
    cos_all = jnp.cos(child_angle)[:, :, None]
    sin_all = jnp.sin(child_angle)[:, :, None]
    split_radiation = radiation.reshape(directions, 2, unknowns)
    leaf_halves = jnp.einsum(
        "qcj,bjr->bcqr", split_radiation, currents, preferred_element_type=jnp.float32
    )
    leaf_terms = leaf_halves[:, 0] + turned(leaf_halves[:, 1])
    rotated = cos_all * leaf_terms + sin_all * turned(leaf_terms)
    local_pattern = jnp.sum(
        rotated.reshape(parents_dev, CHILD, directions, 2 * rhs_width), axis=1
    ).astype(jnp.bfloat16)
    group_slice = lax.all_to_all(local_pattern, "dir", split_axis=1, concat_axis=0, tiled=True)
    src_rows = lax.dynamic_slice_in_dim(inter_src, group_first, group_size, 0)
    off_rows = lax.dynamic_slice_in_dim(inter_off, group_first, group_size, 0)
    count_rows = lax.dynamic_slice_in_dim(inter_count, group_first, group_size, 0)
    pieces = lax.all_gather(group_slice, "box", axis=0, tiled=True)
    coef = coefficients(
        translation, src_rows, off_rows, count_rows, pieces.shape[0], dir_start, dir_width
    )
    incoming_slice = apply_coef(coef, pieces).astype(jnp.bfloat16)
    incoming = lax.all_to_all(incoming_slice, "dir", split_axis=0, concat_axis=1, tiled=True)
    incoming_full = jnp.repeat(incoming, CHILD, axis=0).astype(jnp.float32)
    shifted = (cos_all * incoming_full - sin_all * turned(incoming_full)).astype(jnp.bfloat16)
    mixed_terms = jnp.einsum("qj,bqr->bjr", radiation, shifted, preferred_element_type=jnp.float32)
    far_real = mixed_terms[:, :unknowns, :rhs_width] + mixed_terms[:, unknowns:, rhs_width:]
    far_imag = mixed_terms[:, :unknowns, rhs_width:] - mixed_terms[:, unknowns:, :rhs_width]
    far_part = jnp.concatenate([far_real, far_imag], axis=-1)
    return (near_part + far_part).astype(jnp.bfloat16)


def solution(mesh):
    return jax.shard_map(
        local,
        mesh=mesh,
        in_specs=(
            P(("box", "dir"), None, None),
            P(("box", "dir"), None, None, None),
            P(("box", "dir"), None),
            P(("box", "dir")),
            P(),
            P(("box", "dir"), None),
            P(),
            P(),
            P(),
            P(),
        ),
        out_specs=P(("box", "dir"), None, None),
        check_vma=False,
    )
```

profile of v0, /device:TPU:1, one launch (start us, length us, event | category | flops | bytes accessed | tf_op | source)
XLA Modules:
  0.0 186.5 jit_solution(17364101178362907800)
XLA Ops:
  6.5 3.7 %convolution_bitcast_fusion = f32[16,2,1024,128]{2,3,1,0:T(8,128)S(1)} fusion(bf16[16,128,128]{2,1,0:T(8,128)(2,1)} %param.10, bf16[1024,256]{1,0:T(8,128)(2,1)} %param.14), kind=kOutput, calls=%fused_computation.2 | convolution fusion | flops 1073741824 | bytes 17825792 | tf_op jit(solution)/shard_map/qcj,bjr->bcqr/dot_general | solution.py:101
  10.3 5.7 %copy-done.2 = f32[16,2,1024,128]{2,3,1,0:T(8,128)} copy-done((f32[16,2,1024,128]{2,3,1,0:T(8,128)}, f32[16,2,1024,128]{2,3,1,0:T(8,128)S(1)}, u32[]{:S(2)}) %copy-start.2) | copy-done | bytes 16777240
  16.0 4.1 %slice_bitcast_fusion = f32[16,1024,128]{1,2,0:T(8,128)} fusion(f32[16,2,1024,128]{2,3,1,0:T(8,128)S(1)} %convolution_bitcast_fusion), kind=kLoop, calls=%fused_computation.6 | loop fusion | bytes 16777216 | tf_op jit(solution)/shard_map/squeeze | solution.py:104
  20.1 10.6 %slice_negate_fusion.1 = (f32[16,1024,64]{1,2,0:T(8,128)}, f32[1,16,1024,64]{2,3,1,0:T(8,128)}, f32[1,16,1024,64]{2,3,1,0:T(8,128)}, f32[16,1024,64]{1,2,0:T(8,128)}) fusion(f32[16,1024,128]{1,2,0:T(8,128)} %slice_bitcast_fusion), kind=kLoop, calls=%fused_computation.19 | loop fusion | flops 1048576 | bytes 25165824 | tf_op jit(solution)/shard_map/neg | solution.py:28
  30.7 6.8 %maximum_add_fusion.1 = f32[16,1024,128]{1,2,0:T(8,128)S(1)} fusion(f32[16,1024,64]{1,2,0:T(8,128)} %get-tuple-element.14, f32[16,1024,64]{1,2,0:T(8,128)} %get-tuple-element.11, f32[16,2,1024,128]{2,3,1,0:T(8,128)} %copy-done.2), kind=kLoop, calls=%fused_computation.11 | loop fusion | flops 4194304 | bytes 25165824 | tf_op jit(solution)/shard_map/add | solution.py:104
  37.6 5.1 %fusion.8 = (f32[1,16,1024,64]{2,3,1,0:T(8,128)}, f32[1,16,1024,64]{2,3,1,0:T(8,128)}) fusion(f32[16,1024,128]{1,2,0:T(8,128)S(1)} %maximum_add_fusion.1), kind=kLoop, calls=%fused_computation.18 | loop fusion | flops 1048576 | bytes 16777216 | tf_op jit(solution)/shard_map/concatenate | solution.py:28
  42.7 0.2 fusion.47
  42.9 1.0 copy-done.5
  43.9 7.7 %fusion.5 = bf16[1024,128]{0,1:T(8,128)(2,1)S(1)} fusion(f32[1,16,1024,64]{2,3,1,0:T(8,128)S(1)} %copy-done.5, f32[1,16,1024,64]{2,3,1,0:T(8,128)S(1)} %copy-done.4, f32[1,16,1024,64]{2,3,1,0:T(8,128)} %get-tuple-element.10, f32[1,16,1024,64]{2,3,1,0:T(8,128)} %get-tuple-element.9, f32[16,2,1024,128]{2,3,1,0:T(8,128)} %copy-done.2, ...), kind=kLoop, calls=%fused_computation.10 | loop fusion | flops 14548992 | bytes 25559040 | tf_op jit(solution)/shard_map/reduce_sum | solution.py:106
  51.7 1.1 copy.81
  52.8 0.5 broadcast.52
  53.3 3.1 %reduce.1 = bf16[1024,128]{1,0:T(8,128)(2,1)S(1)} reduce(bf16[1024,1,128]{2,1,0:T(2,128)(2,1)} %bitcast.108, bf16[]{:T(256)} %broadcast.52), dimensions={1}, to_apply=%bitcast.88.reduce_sub_computation | reduce | bytes 524290
  56.4 0.8 reshape.176
  57.1 12.5 %all_to_all.21 = bf16[8,2,8192]{2,1,0:T(2,128)(2,1)S(1)} all-to-all(bf16[8,2,8192]{2,1,0:T(2,128)(2,1)} %reshape.176), channel_id=1, replica_groups=mesh['box'=16,'dir'=8] {'dir'}, dimensions={0} | all-to-all | bytes 524288 | tf_op jit(solution)/shard_map/all_to_all | solution.py:109
  69.6 1.0 reshape.177
  70.6 1.8 copy.103
  72.4 0.0 all-gather.2.cloned.1.call-update
  72.4 0.9 fusion.46
  73.3 3.1 %collective-permute-start = (bf16[8,128,128]{2,1,0:T(8,128)(2,1)}, bf16[8,128,128]{2,1,0:T(8,128)(2,1)}, u32[]{:S(2)}, u32[]{:S(2)}) collective-permute-start(bf16[8,128,128]{2,1,0:T(8,128)(2,1)} %get-tuple-element.23), channel_id=1, source_target_pairs={{0,1},{1,2},{2,3},{3,4},{4,5},{5,6},{6,7},{7,8},{8,9},{9,10},{10,1... | collective-permute-start | bytes 786440 | tf_op jit(solution)/shard_map/ppermute | solution.py:17
  76.4 2.1 %collective-permute-start.1 = (bf16[8,128,128]{2,1,0:T(8,128)(2,1)}, bf16[8,128,128]{2,1,0:T(8,128)(2,1)}, u32[]{:S(2)}, u32[]{:S(2)}) collective-permute-start(bf16[8,128,128]{2,1,0:T(8,128)(2,1)} %get-tuple-element.24), channel_id=1, source_target_pairs={{1,0},{2,1},{3,2},{4,3},{5,4},{6,5},{7,6},{8,7},{9,8},{10,9},{11,1... | collective-permute-start | bytes 786440 | tf_op jit(solution)/shard_map/ppermute | solution.py:19
  78.5 0.1 compare_and_fusion
  78.6 0.1 copy.85
  78.7 0.1 reshape.156
  78.8 0.1 copy.84
  78.9 0.1 constant_dynamic-slice_fusion.1
  78.9 0.1 copy.83
  79.0 0.1 dynamic_slice.13
  79.1 1.0 gather_fusion.1
  80.1 0.1 iota_compare_fusion.1
  80.2 0.8 fusion.33
  81.0 0.1 slice_bitcast_fusion.4
  81.1 1.0 copy.87
  82.1 1.0 copy.89
  83.1 0.1 copy.74
  83.2 0.1 reshape.148
  83.3 0.1 copy.73
  83.4 1.0 collective-permute-done.1
  84.4 1.2 pad_maximum_fusion
  85.6 3.1 %gather_fusion = bf16[128,128,128]{2,1,0:T(8,128)(2,1)} fusion(bf16[32,128,128]{2,1,0:T(8,128)(2,1)S(1)} %pad_maximum_fusion, s32[1024]{0:T(1024)S(1)} %pad_clamp_fusion.1), kind=kCustom, calls=%fused_computation | custom fusion | bytes 8389120 | tf_op jit(solution)/shard_map/jit(_take)/gather | solution.py:92
  88.6 6.5 %copy.75 = bf16[16,8,128,128]{2,3,1,0:T(8,128)(2,1)} copy(bf16[16,8,128,128]{3,2,1,0:T(8,128)(2,1)} %bitcast.105) | data formatting | bytes 8388608 | tf_op jit(solution)/shard_map/jit(_take)/gather | solution.py:92
  95.1 8.8 %fusion.15 = f32[16,2,128,128]{2,3,1,0:T(8,128)} fusion(bf16[16,8,128,128]{2,3,1,0:T(8,128)(2,1)} %copy.75, pred[16,8]{1,0:T(8,128)(4,1)S(1)} %copy.73, bf16[16,8,128,256]{3,2,1,0:T(8,128)(2,1)} %param.11), kind=kOutput, calls=%fused_computation.25 | convolution fusion | flops 1075838976 | bytes 14680192 | tf_op jit(solution)/shard_map/bkpcj,bkjr->bcpr/dot_general | solution.py:94
  103.9 22.3 %all-gather.2.cloned.1.call-done = bf16[128,128,128]{2,1,0:T(8,128)(2,1)} async-done(((bf16[8,128,128]{2,1,0:T(8,128)(2,1)}), bf16[128,128,128]{2,1,0:T(8,128)(2,1)}) %all-gather.2.cloned.1.call-update) | async-done | bytes 4194320 | tf_op jit(solution)/shard_map/all_gather | solution.py:113
  126.2 7.5 %fusion.45 = (bf16[128,128,64]{2,1,0:T(8,128)(2,1)}, bf16[128,128,64]{2,1,0:T(8,128)(2,1)}) fusion(bf16[128,128,128]{2,1,0:T(8,128)(2,1)} %all-gather.2.cloned.1.call-done), kind=kLoop, calls=%fused_computation.76 | loop fusion | bytes 8388608 | tf_op jit(solution)/shard_map/slice | solution.py:47
  133.8 5.6 %copy.106 = bf16[128,128,64]{0,2,1:T(8,128)(2,1)S(1)} copy(bf16[128,128,64]{2,1,0:T(8,128)(2,1)} %get-tuple-element.15) | data formatting | bytes 4194304
  139.4 6.6 %copy.107 = bf16[128,128,64]{0,2,1:T(8,128)(2,1)} copy(bf16[128,128,64]{2,1,0:T(8,128)(2,1)} %get-tuple-element.16) | data formatting | bytes 4194304
  146.0 3.3 %fusion.48 = f32[128,64,8]{1,2,0:T(8,128)S(1)} fusion(bf16[128,128,64]{0,2,1:T(8,128)(2,1)S(1)} %copy.106, f32[8,128,128]{1,0,2:T(8,128)S(1)} %copy-done.8), kind=kOutput, calls=%fused_computation.79 | convolution fusion | flops 100663296 | bytes 2883584 | tf_op jit(solution)/shard_map/tsq,sqr->tqr/dot_general | solution.py:51
  149.4 4.9 %fusion.49 = f32[128,64,8]{1,2,0:T(8,128)S(1)} fusion(bf16[128,128,64]{0,2,1:T(8,128)(2,1)} %copy.107, f32[8,128,128]{1,0,2:T(8,128)S(1)} %copy-done.8), kind=kOutput, calls=%fused_computation.80 | convolution fusion | flops 100663296 | bytes 2883584 | tf_op jit(solution)/shard_map/tsq,sqr->tqr/dot_general | solution.py:54
  154.3 3.4 %fusion.26 = bf16[8,128,64]{2,0,1:T(8,128)(2,1)S(1)} fusion(f32[128,64,8]{1,2,0:T(8,128)S(1)} %fusion.48, bf16[128,128,64]{0,2,1:T(8,128)(2,1)S(1)} %copy-done.3, f32[8,128,128]{1,0,2:T(8,128)S(1)} %copy-done.7), kind=kOutput, calls=%fused_computation.32 | convolution fusion | flops 100794368 | bytes 3014656 | tf_op jit(solution)/shard_map/tsq,sqr->tqr/dot_general | solution.py:51
  157.7 3.4 %fusion.25 = bf16[8,128,64]{2,0,1:T(8,128)(2,1)S(1)} fusion(f32[128,64,8]{1,2,0:T(8,128)S(1)} %fusion.49, bf16[128,128,64]{0,2,1:T(8,128)(2,1)S(1)} %copy.106, f32[8,128,128]{1,0,2:T(8,128)S(1)} %copy-done.7), kind=kOutput, calls=%fused_computation.31 | convolution fusion | flops 100794368 | bytes 3014656 | tf_op jit(solution)/shard_map/tsq,sqr->tqr/dot_general | solution.py:54
  161.0 0.2 pad_maximum_fusion.1
  161.2 0.7 copy.92
  162.0 5.0 %all-to-all-start.1 = ((bf16[8,128,128]{2,1,0:T(8,128)(2,1)}), bf16[8,128,128]{2,1,0:T(8,128)(2,1)S(1)}, u32[]{:S(2)}, u32[]{:S(2)}) async-start(bf16[8,128,128]{2,1,0:T(8,128)(2,1)} %copy.92), calls=%async_computation.1 | async-start | bytes 524288 | tf_op jit(solution)/shard_map/all_to_all | solution.py:118
  166.9 2.3 %slice_bitcast_fusion.2 = f32[16,128,128]{1,2,0:T(8,128)} fusion(f32[16,2,128,128]{2,3,1,0:T(8,128)} %fusion.15), kind=kLoop, calls=%fused_computation.33 | loop fusion | bytes 2097152 | tf_op jit(solution)/shard_map/squeeze | solution.py:97
  169.2 4.2 %all-to-all-done.1 = bf16[8,128,128]{2,1,0:T(8,128)(2,1)S(1)} async-done(((bf16[8,128,128]{2,1,0:T(8,128)(2,1)}), bf16[8,128,128]{2,1,0:T(8,128)(2,1)S(1)}, u32[]{:S(2)}, u32[]{:S(2)}) %all-to-all-start.1) | async-done | bytes 262176 | tf_op jit(solution)/shard_map/all_to_all | solution.py:118
  173.4 0.1 bitcast_convert_fusion
  173.5 0.2 copy.93
  173.7 0.2 copy.95
  173.9 0.5 reshape.143
  174.4 0.5 reshape.144
  175.0 1.8 fusion.20
  176.8 0.3 slice_add_fusion
  177.1 1.3 copy-done.10
  178.4 0.2 fusion.29
  178.6 1.0 copy.96
  (48 shorter events, 0.2 us)
Async XLA Ops:
  6.5 72.6 %copy-start = (f32[316,2,1024]{2,1,0:T(2,128)S(1)}, f32[316,2,1024]{2,1,0:T(2,128)}, u32[]{:S(2)}) copy-start(f32[316,2,1024]{2,1,0:T(2,128)} %param.16) | copy-start | bytes 7766020
  6.5 119.7 %all-gather.2.cloned.1.call-start = ((), (), s32[]{:S(2)}) async-start(), calls=%async_computation.2 | async-start | bytes 4456448 | tf_op jit(solution)/shard_map/all_gather | solution.py:113
  10.3 5.7 %copy-start.2 = (f32[16,2,1024,128]{2,3,1,0:T(8,128)}, f32[16,2,1024,128]{2,3,1,0:T(8,128)S(1)}, u32[]{:S(2)}) copy-start(f32[16,2,1024,128]{2,3,1,0:T(8,128)S(1)} %convolution_bitcast_fusion) | copy-start | bytes 50331652
  37.5 5.1 %copy-start.16 = (f32[16,1024]{1,0:T(8,128)S(1)}, f32[16,1024]{1,0:T(8,128)}, u32[]{:S(2)}) copy-start(f32[16,1024]{1,0:T(8,128)} %param.15) | copy-start | bytes 196612
  37.5 5.4 %copy-start.4 = (f32[1,16,1024,64]{2,3,1,0:T(8,128)S(1)}, f32[1,16,1024,64]{2,3,1,0:T(8,128)}, u32[]{:S(2)}) copy-start(f32[1,16,1024,64]{2,3,1,0:T(8,128)} %get-tuple-element.12) | copy-start | bytes 12582916
  37.5 6.4 %copy-start.5 = (f32[1,16,1024,64]{2,3,1,0:T(8,128)S(1)}, f32[1,16,1024,64]{2,3,1,0:T(8,128)}, u32[]{:S(2)}) copy-start(f32[1,16,1024,64]{2,3,1,0:T(8,128)} %get-tuple-element.13) | copy-start | bytes 12582916
  42.9 8.8 %copy-start.12 = (f32[16,1024]{1,0:T(8,128)}, f32[16,1024]{1,0:T(8,128)S(1)}, u32[]{:S(2)}) copy-start(f32[16,1024]{1,0:T(8,128)S(1)} %get-tuple-element.25) | copy-start | bytes 196612
  42.9 8.8 %copy-start.14 = (f32[16,1024]{1,0:T(8,128)}, f32[16,1024]{1,0:T(8,128)S(1)}, u32[]{:S(2)}) copy-start(f32[16,1024]{1,0:T(8,128)S(1)} %get-tuple-element.26) | copy-start | bytes 196612
  51.7 20.7 %copy-start.6 = (bf16[16,128,128]{2,1,0:T(8,128)(2,1)S(1)}, bf16[16,128,128]{2,1,0:T(8,128)(2,1)}, u32[]{:S(2)}) copy-start(bf16[16,128,128]{2,1,0:T(8,128)(2,1)} %param.10) | copy-start | bytes 1572868
  51.7 26.8 %copy-start.17 = (s32[128,6]{0,1:T(8,128)S(1)}, s32[128,6]{0,1:T(8,128)}, u32[]{:S(2)}) copy-start(s32[128,6]{0,1:T(8,128)} %param.18) | copy-start | bytes 9220
  51.7 27.2 %copy-start.18 = (s32[128,6]{0,1:T(8,128)S(1)}, s32[128,6]{0,1:T(8,128)}, u32[]{:S(2)}) copy-start(s32[128,6]{0,1:T(8,128)} %param.17) | copy-start | bytes 9220
  51.7 27.3 %copy-start.21 = (s32[128]{0:T(128)S(1)}, s32[128]{0:T(128)}, u32[]{:S(2)}) copy-start(s32[128]{0:T(128)} %param.19) | copy-start | bytes 1540
  70.6 12.5 %copy-start.19 = (s32[16,8]{0,1:T(8,128)S(1)}, s32[16,8]{0,1:T(8,128)}, u32[]{:S(2)}) copy-start(s32[16,8]{0,1:T(8,128)} %param.12) | copy-start | bytes 1540
  70.6 12.5 %copy-start.20 = (s32[16]{0:T(128)S(1)}, s32[16]{0:T(128)}, u32[]{:S(2)}) copy-start(s32[16]{0:T(128)} %param.13) | copy-start | bytes 196
  73.3 10.1 %collective-permute-start = (bf16[8,128,128]{2,1,0:T(8,128)(2,1)}, bf16[8,128,128]{2,1,0:T(8,128)(2,1)}, u32[]{:S(2)}, u32[]{:S(2)}) collective-permute-start(bf16[8,128,128]{2,1,0:T(8,128)(2,1)} %get-tuple-element.23), channel_id=1, source_target_pairs={{0,1},{1,2},{2,3},{3,4},{4,5},{5,6},{6,7},{7,8},{8,9},{9,10},{10,1... | collective-permute-start | bytes 786440 | tf_op jit(solution)/shard_map/ppermute | solution.py:17
  76.4 8.0 %collective-permute-start.1 = (bf16[8,128,128]{2,1,0:T(8,128)(2,1)}, bf16[8,128,128]{2,1,0:T(8,128)(2,1)}, u32[]{:S(2)}, u32[]{:S(2)}) collective-permute-start(bf16[8,128,128]{2,1,0:T(8,128)(2,1)} %get-tuple-element.24), channel_id=1, source_target_pairs={{1,0},{2,1},{3,2},{4,3},{5,4},{6,5},{7,6},{8,7},{9,8},{10,9},{11,1... | collective-permute-start | bytes 786440 | tf_op jit(solution)/shard_map/ppermute | solution.py:19
  139.4 6.6 %copy-start.8 = (f32[8,128,128]{1,0,2:T(8,128)S(1)}, f32[8,128,128]{1,0,2:T(8,128)}, u32[]{:S(2)}) copy-start(f32[8,128,128]{1,0,2:T(8,128)} %copy.87) | copy-start | bytes 1572868
  146.0 8.3 %copy-start.3 = (bf16[128,128,64]{0,2,1:T(8,128)(2,1)S(1)}, bf16[128,128,64]{0,2,1:T(8,128)(2,1)}, u32[]{:S(2)}) copy-start(bf16[128,128,64]{0,2,1:T(8,128)(2,1)} %copy.107) | copy-start | bytes 6291460
  146.0 8.3 %copy-start.7 = (f32[8,128,128]{1,0,2:T(8,128)S(1)}, f32[8,128,128]{1,0,2:T(8,128)}, u32[]{:S(2)}) copy-start(f32[8,128,128]{1,0,2:T(8,128)} %copy.89) | copy-start | bytes 1572868
  162.0 11.5 %all-to-all-start.1 = ((bf16[8,128,128]{2,1,0:T(8,128)(2,1)}), bf16[8,128,128]{2,1,0:T(8,128)(2,1)S(1)}, u32[]{:S(2)}, u32[]{:S(2)}) async-start(bf16[8,128,128]{2,1,0:T(8,128)(2,1)} %copy.92), calls=%async_computation.1 | async-start | bytes 524288 | tf_op jit(solution)/shard_map/all_to_all | solution.py:118
  173.9 1.1 copy-start.11
  173.9 1.1 copy-start.13
  173.9 1.1 copy-start.15
  175.0 1.8 copy-start.9
  175.0 4.6 %copy-start.1 = (f32[316,2,1024]{2,1,0:T(2,128)S(1)}, f32[316,2,1024]{2,1,0:T(2,128)}, u32[]{:S(2)}) copy-start(f32[316,2,1024]{2,1,0:T(2,128)} %param.16) | copy-start | bytes 7766020
  176.8 1.6 copy-start.10
Sparse Core Ops, SparseCore 0:
  72.5 53.6 all-gather.1
where the time goes:
time: 187 us; the launch traced here: 186 us
  local copies, waits for them, and re-layouts  57.1 us (31%)
  other arithmetic  35.3 us (19%)
  matrix products  30.1 us (16%)
  waiting for transfers between devices  27.6 us (15%)
  between operations  13.8 us (7%)
  blocking collectives  12.5 us (7%)
  starting transfers between devices  10.2 us (5%)
    unnamed x50, local copies, waits for them, and re-layouts  24.4 us
    all_gather x1, waiting for transfers between devices, local(): pieces = lax.all_gather(group_slice, 'box', axis=0, tiled=True)  22.3 us
    all_to_all x1, blocking collectives, local(): lax.all_to_all(local_pattern, 'dir', split_axis=1, concat_axis=0, tiled=T...  12.5 us
    neg x2, other arithmetic, turned(): -values[..., half_width:]  10.6 us
    gather x2, local copies, waits for them, and re-layouts, local(): jnp.take(extended, local_ids, axis=0, mode='fill', fill_value=0)  9.57 us
    dot_general x1, matrix products, local(): jnp.einsum('bkpcj,bkjr->bcpr', split_blocks, neighbours, preferred_elemen...  8.8 us
    reduce_sum x1, other arithmetic, local(): jnp.sum(rotated.reshape(parents_dev, CHILD, directions, 2 * rhs_width), a...  7.71 us
    slice x1, local copies, waits for them, and re-layouts, apply_coef(): real_part = pieces_full[..., :half_width]  7.51 us
  transfers between devices with their start and end apart: 4, of which 3 were waited for; matrix products, arithmetic and copies ran while one was open for 15% of the time, Pallas kernels for 0%

commit v1 on v0

--- a/solution.py
+++ b/solution.py
@@ -4,6 +4,24 @@
 from jax.sharding import PartitionSpec as P
 
 CHILD = 16
+
+
+def joined_along(tiles, dim):
+    tiles = jnp.moveaxis(tiles, 0, dim)
+    shape = tiles.shape
+    return tiles.reshape(*shape[:dim], shape[dim] * shape[dim + 1], *shape[dim + 2 :])
+
+
+def doubled(shard, axis):
+    peers = lax.axis_size(axis)
+    pieces = shard[None]
+    for level in range(peers.bit_length() - 1):
+        bit = 1 << level
+        theirs = lax.ppermute(pieces, axis, [(i, i ^ bit) for i in range(peers)])
+        both = jnp.stack([pieces, theirs])
+        upper = lax.axis_index(axis) >> level & 1
+        pieces = jnp.where(upper == 0, both, both[::-1]).reshape(-1, *shard.shape)
+    return pieces
 
 
 def padded(cells, sides, width):
@@ -110,7 +128,7 @@
     src_rows = lax.dynamic_slice_in_dim(inter_src, group_first, group_size, 0)
     off_rows = lax.dynamic_slice_in_dim(inter_off, group_first, group_size, 0)
     count_rows = lax.dynamic_slice_in_dim(inter_count, group_first, group_size, 0)
-    pieces = lax.all_gather(group_slice, "box", axis=0, tiled=True)
+    pieces = joined_along(doubled(group_slice, "box"), 0)
     coef = coefficients(
         translation, src_rows, off_rows, count_rows, pieces.shape[0], dir_start, dir_width
     )

time: 187 us -> 220 us (1.18)
  waiting for transfers between devices: 27.6 us -> 53.1 us
  starting transfers between devices: 10.2 us -> 23.9 us
  between operations: 13.8 us -> 0.45 us
  other arithmetic: 35.3 us -> 47.2 us
  local copies, waits for them, and re-layouts: 57.1 us -> 51.6 us
    ppermute x0 -> x4, waiting for transfers between devices: none -> 48.9 us  [doubled(): theirs = lax.ppermute(pieces, axis, [(i, i ^ bit) for i in range(peers)])]
    all_gather x1 -> x0, waiting for transfers between devices: 22.3 us -> none  [local(): pieces = lax.all_gather(group_slice, 'box', axis=0, tiled=True)]
    ppermute x0 -> x4, starting transfers between devices: none -> 8.99 us  [doubled(): theirs = lax.ppermute(pieces, axis, [(i, i ^ bit) for i in range(peers)])]
    another operation x0 -> x5, other arithmetic: none -> 7.86 us  [doubled(): both = jnp.stack([pieces, theirs])]
    select_n x0 -> x3, other arithmetic: none -> 4.91 us  [doubled(): pieces = jnp.where(upper == 0, both, both[::-1]).reshape(-1, *shard.shape)]
    slice x1, local copies, waits for them, and re-layouts: 7.51 us -> 4.22 us  [apply_coef(): real_part = pieces_full[..., :half_width]]
    all_to_all x1, starting transfers between devices: 4.96 us -> 7.76 us  [local(): lax.all_to_all(incoming_slice, 'dir', split_axis=0, concat_axis=1, tiled=...]
  transfers between devices with their start and end apart: 4 -> 7, of which waited for: 3 -> 5; matrix products, arithmetic and copies ran while one was open for 15% -> 14% of each run, Pallas kernels for 0% -> 0%
where the time goes in v1:
time: 220 us; the launch traced here: 219 us
  waiting for transfers between devices  53.1 us (24%)
  local copies, waits for them, and re-layouts  51.6 us (23%)
  other arithmetic  47.2 us (21%)
  matrix products  30.1 us (14%)
  starting transfers between devices  23.9 us (11%)
  blocking collectives  12.3 us (6%)
    ppermute x4, waiting for transfers between devices, doubled(): theirs = lax.ppermute(pieces, axis, [(i, i ^ bit) for i in range(peers)])  48.9 us
    unnamed x50, local copies, waits for them, and re-layouts  23 us
    all_to_all x1, blocking collectives, local(): lax.all_to_all(local_pattern, 'dir', split_axis=1, concat_axis=0, tiled=T...  12.3 us
    neg x2, other arithmetic, turned(): -values[..., half_width:]  10.6 us
    gather x2, local copies, waits for them, and re-layouts, local(): jnp.take(extended, local_ids, axis=0, mode='fill', fill_value=0)  9.51 us
    ppermute x4, starting transfers between devices, doubled(): theirs = lax.ppermute(pieces, axis, [(i, i ^ bit) for i in range(peers)])  8.99 us
    dot_general x1, matrix products, local(): jnp.einsum('bkpcj,bkjr->bcpr', split_blocks, neighbours, preferred_elemen...  8.86 us
    another operation x5, other arithmetic, doubled(): both = jnp.stack([pieces, theirs])  7.86 us
  transfers between devices with their start and end apart: 7, of which 5 were waited for; matrix products, arithmetic and copies ran while one was open for 14% of the time, Pallas kernels for 0%

profile of v1, /device:TPU:1, one launch (start us, length us, event | category | flops | bytes accessed | tf_op | source)
XLA Modules:
  0.0 218.7 jit_solution(9531685528766841050)
XLA Ops:
  0.0 3.7 %convolution_bitcast_fusion = f32[16,2,1024,128]{2,3,1,0:T(8,128)S(1)} fusion(bf16[16,128,128]{2,1,0:T(8,128)(2,1)} %param.10, bf16[1024,256]{1,0:T(8,128)(2,1)} %param.14), kind=kOutput, calls=%fused_computation.2 | convolution fusion | flops 1073741824 | bytes 17825792 | tf_op jit(solution)/shard_map/qcj,bjr->bcqr/dot_general | solution.py:119
  3.7 5.7 %copy-done.2 = f32[16,2,1024,128]{2,3,1,0:T(8,128)} copy-done((f32[16,2,1024,128]{2,3,1,0:T(8,128)}, f32[16,2,1024,128]{2,3,1,0:T(8,128)S(1)}, u32[]{:S(2)}) %copy-start.2) | copy-done | bytes 16777240
  9.5 4.1 %slice_bitcast_fusion = f32[16,1024,128]{1,2,0:T(8,128)} fusion(f32[16,2,1024,128]{2,3,1,0:T(8,128)S(1)} %convolution_bitcast_fusion), kind=kLoop, calls=%fused_computation.6 | loop fusion | bytes 16777216 | tf_op jit(solution)/shard_map/squeeze | solution.py:122
  13.6 10.6 %slice_negate_fusion.1 = (f32[16,1024,64]{1,2,0:T(8,128)}, f32[1,16,1024,64]{2,3,1,0:T(8,128)}, f32[1,16,1024,64]{2,3,1,0:T(8,128)}, f32[16,1024,64]{1,2,0:T(8,128)}) fusion(f32[16,1024,128]{1,2,0:T(8,128)} %slice_bitcast_fusion), kind=kLoop, calls=%fused_computation.20 | loop fusion | flops 1048576 | bytes 25165824 | tf_op jit(solution)/shard_map/neg | solution.py:46
  24.2 6.8 %maximum_add_fusion.1 = f32[16,1024,128]{1,2,0:T(8,128)S(1)} fusion(f32[16,1024,64]{1,2,0:T(8,128)} %get-tuple-element.14, f32[16,1024,64]{1,2,0:T(8,128)} %get-tuple-element.11, f32[16,2,1024,128]{2,3,1,0:T(8,128)} %copy-done.2), kind=kLoop, calls=%fused_computation.11 | loop fusion | flops 4194304 | bytes 25165824 | tf_op jit(solution)/shard_map/add | solution.py:122
  31.1 5.1 %fusion.8 = (f32[1,16,1024,64]{2,3,1,0:T(8,128)}, f32[1,16,1024,64]{2,3,1,0:T(8,128)}) fusion(f32[16,1024,128]{1,2,0:T(8,128)S(1)} %maximum_add_fusion.1), kind=kLoop, calls=%fused_computation.19 | loop fusion | flops 1048576 | bytes 16777216 | tf_op jit(solution)/shard_map/concatenate | solution.py:46
  36.2 0.2 fusion.49
  36.4 1.0 copy-done.5
  37.4 7.7 %fusion.5 = bf16[1024,128]{0,1:T(8,128)(2,1)S(1)} fusion(f32[1,16,1024,64]{2,3,1,0:T(8,128)S(1)} %copy-done.5, f32[1,16,1024,64]{2,3,1,0:T(8,128)S(1)} %copy-done.4, f32[1,16,1024,64]{2,3,1,0:T(8,128)} %get-tuple-element.10, f32[1,16,1024,64]{2,3,1,0:T(8,128)} %get-tuple-element.9, f32[16,2,1024,128]{2,3,1,0:T(8,128)} %copy-done.2, ...), kind=kLoop, calls=%fused_computation.10 | loop fusion | flops 14548992 | bytes 25559040 | tf_op jit(solution)/shard_map/reduce_sum | solution.py:124
  45.2 0.4 copy.83
  45.6 0.5 broadcast.52
  46.1 2.2 %reduce.1 = bf16[1024,128]{1,0:T(8,128)(2,1)S(1)} reduce(bf16[1024,1,128]{2,1,0:T(2,128)(2,1)S(1)} %bitcast.123, bf16[]{:T(256)} %broadcast.52), dimensions={1}, to_apply=%bitcast.102.reduce_sub_computation | reduce | bytes 524290
  48.4 12.3 %all_to_all.8 = bf16[8,2,8192]{2,1,0:T(2,128)(2,1)S(1)} all-to-all(bf16[8,2,8192]{2,1,0:T(2,128)(2,1)S(1)} %reshape.191), channel_id=1, replica_groups=mesh['box'=16,'dir'=8] {'dir'}, dimensions={0} | all-to-all | bytes 524288 | tf_op jit(solution)/shard_map/all_to_all | solution.py:127
  60.6 1.0 reshape.192
  61.6 1.1 copy.105
  62.7 1.3 collective-permute-start.2
  64.0 5.6 %collective-permute-done.2 = bf16[1,8,128,128]{3,2,1,0:T(8,128)(2,1)} collective-permute-done((bf16[1,8,128,128]{3,2,1,0:T(8,128)(2,1)S(1)}, bf16[1,8,128,128]{3,2,1,0:T(8,128)(2,1)}, u32[]{:S(2)}, u32[]{:S(2)}) %collective-permute-start.2) | collective-permute-done | bytes 262176 | tf_op jit(solution)/shard_map/ppermute | solution.py:20
  69.7 1.0 pad_maximum_fusion.4
  70.7 1.2 fusion.34
  71.9 2.8 %collective-permute-start.3 = (bf16[2,8,128,128]{3,2,1,0:T(8,128)(2,1)}, bf16[2,8,128,128]{3,2,1,0:T(8,128)(2,1)}, u32[]{:S(2)}, u32[]{:S(2)}) collective-permute-start(bf16[2,8,128,128]{3,2,1,0:T(8,128)(2,1)} %get-tuple-element.24), channel_id=1, source_target_pairs={{0,16},{8,24},{16,0},{24,8},{32,48},{40,56},{48,32},{56,40},{64,80... | collective-permute-start | bytes 1572872 | tf_op jit(solution)/shard_map/ppermute | solution.py:20
  74.6 10.5 %collective-permute-done.3 = bf16[2,8,128,128]{3,2,1,0:T(8,128)(2,1)} collective-permute-done((bf16[2,8,128,128]{3,2,1,0:T(8,128)(2,1)}, bf16[2,8,128,128]{3,2,1,0:T(8,128)(2,1)}, u32[]{:S(2)}, u32[]{:S(2)}) %collective-permute-start.3) | collective-permute-done | bytes 524320 | tf_op jit(solution)/shard_map/ppermute | solution.py:20
  85.1 1.3 pad_maximum_fusion.3
  86.4 1.2 reverse_select_fusion.2
  87.7 1.6 collective-permute-start.4
  89.3 0.8 fusion.48
  90.2 5.2 %collective-permute-start = (bf16[8,128,128]{2,1,0:T(8,128)(2,1)}, bf16[8,128,128]{2,1,0:T(8,128)(2,1)}, u32[]{:S(2)}, u32[]{:S(2)}) collective-permute-start(bf16[8,128,128]{2,1,0:T(8,128)(2,1)} %get-tuple-element.25), channel_id=1, source_target_pairs={{0,1},{1,2},{2,3},{3,4},{4,5},{5,6},{6,7},{7,8},{8,9},{9,10},{10,1... | collective-permute-start | bytes 786440 | tf_op jit(solution)/shard_map/ppermute | solution.py:35
  95.4 1.9 collective-permute-start.1
  97.8 14.3 %collective-permute-done.4 = bf16[4,8,128,128]{3,2,1,0:T(8,128)(2,1)} collective-permute-done((bf16[4,8,128,128]{3,2,1,0:T(8,128)(2,1)}, bf16[4,8,128,128]{3,2,1,0:T(8,128)(2,1)}, u32[]{:S(2)}, u32[]{:S(2)}) %collective-permute-start.4) | collective-permute-done | bytes 1048608 | tf_op jit(solution)/shard_map/ppermute | solution.py:20
  112.0 1.7 pad_maximum_fusion.1
  113.8 1.9 reverse_select_fusion.1
  115.7 3.3 %collective-permute-start.5 = (bf16[8,8,128,128]{3,2,1,0:T(8,128)(2,1)}, bf16[8,8,128,128]{3,2,1,0:T(8,128)(2,1)}, u32[]{:S(2)}, u32[]{:S(2)}) collective-permute-start(bf16[8,8,128,128]{3,2,1,0:T(8,128)(2,1)} %bitcast.28), channel_id=1, source_target_pairs={{0,64},{8,72},{16,80},{24,88},{32,96},{40,104},{48,112},{56,120},{... | collective-permute-start | bytes 6291464 | tf_op jit(solution)/shard_map/ppermute | solution.py:20
  119.1 0.1 copy.86
  119.3 1.0 gather_fusion.1
  120.3 0.8 fusion.35
  121.2 1.0 copy.89
  122.2 1.0 copy.91
  123.5 1.2 pad_maximum_fusion.2
  124.7 3.1 %gather_fusion = bf16[128,128,128]{2,1,0:T(8,128)(2,1)} fusion(bf16[32,128,128]{2,1,0:T(8,128)(2,1)S(1)} %pad_maximum_fusion.2, s32[1024]{0:T(1024)S(1)} %pad_clamp_fusion.1), kind=kCustom, calls=%fused_computation | custom fusion | bytes 8389120 | tf_op jit(solution)/shard_map/jit(_take)/gather | solution.py:110
  127.8 6.4 %copy.77 = bf16[16,8,128,128]{2,3,1,0:T(8,128)(2,1)} copy(bf16[16,8,128,128]{3,2,1,0:T(8,128)(2,1)} %bitcast.120) | data formatting | bytes 8388608 | tf_op jit(solution)/shard_map/jit(_take)/gather | solution.py:110
  134.2 8.9 %fusion.15 = f32[16,2,128,128]{2,3,1,0:T(8,128)} fusion(bf16[16,8,128,128]{2,3,1,0:T(8,128)(2,1)} %copy.77, pred[16,8]{1,0:T(8,128)(4,1)S(1)} %copy.75, bf16[16,8,128,256]{3,2,1,0:T(8,128)(2,1)} %param.11), kind=kOutput, calls=%fused_computation.29 | convolution fusion | flops 1075838976 | bytes 14680192 | tf_op jit(solution)/shard_map/bkpcj,bkjr->bcpr/dot_general | solution.py:112
  143.0 18.5 %collective-permute-done.5 = bf16[8,8,128,128]{3,2,1,0:T(8,128)(2,1)} collective-permute-done((bf16[8,8,128,128]{3,2,1,0:T(8,128)(2,1)}, bf16[8,8,128,128]{3,2,1,0:T(8,128)(2,1)}, u32[]{:S(2)}, u32[]{:S(2)}) %collective-permute-start.5) | collective-permute-done | bytes 2097184 | tf_op jit(solution)/shard_map/ppermute | solution.py:20
  161.5 2.6 %pad_maximum_fusion = bf16[2,8,8,128,128]{4,3,2,1,0:T(8,128)(2,1)S(1)} fusion(bf16[1,8,8,128,128]{4,3,2,1,0:T(8,128)(2,1)} %bitcast.29, bf16[1,8,8,128,128]{4,3,2,1,0:T(8,128)(2,1)} %bitcast.27), kind=kLoop, calls=%fused_computation.21 | loop fusion | flops 2097152 | bytes 8388608 | tf_op jit(solution)/shard_map/stack | solution.py:21
  164.1 1.7 reverse_select_fusion
  165.8 4.2 %fusion.47 = (bf16[128,128,64]{2,1,0:T(8,128)(2,1)}, bf16[128,128,64]{2,1,0:T(8,128)(2,1)}) fusion(bf16[128,128,128]{2,1,0:T(8,128)(2,1)S(1)} %bitcast.119), kind=kLoop, calls=%fused_computation.86 | loop fusion | bytes 8388608 | tf_op jit(solution)/shard_map/slice | solution.py:65
  170.1 5.6 %copy.109 = bf16[128,128,64]{0,2,1:T(8,128)(2,1)S(1)} copy(bf16[128,128,64]{2,1,0:T(8,128)(2,1)} %get-tuple-element.15) | data formatting | bytes 4194304
  175.7 6.6 %copy.110 = bf16[128,128,64]{0,2,1:T(8,128)(2,1)} copy(bf16[128,128,64]{2,1,0:T(8,128)(2,1)} %get-tuple-element.16) | data formatting | bytes 4194304
  182.3 3.3 %fusion.50 = f32[128,64,8]{1,2,0:T(8,128)S(1)} fusion(bf16[128,128,64]{0,2,1:T(8,128)(2,1)S(1)} %copy.109, f32[8,128,128]{1,0,2:T(8,128)S(1)} %copy-done.8), kind=kOutput, calls=%fused_computation.89 | convolution fusion | flops 100663296 | bytes 2883584 | tf_op jit(solution)/shard_map/tsq,sqr->tqr/dot_general | solution.py:69
  185.7 4.9 %fusion.51 = f32[128,64,8]{1,2,0:T(8,128)S(1)} fusion(bf16[128,128,64]{0,2,1:T(8,128)(2,1)} %copy.110, f32[8,128,128]{1,0,2:T(8,128)S(1)} %copy-done.8), kind=kOutput, calls=%fused_computation.90 | convolution fusion | flops 100663296 | bytes 2883584 | tf_op jit(solution)/shard_map/tsq,sqr->tqr/dot_general | solution.py:72
  190.6 3.4 %fusion.26 = bf16[8,128,64]{2,0,1:T(8,128)(2,1)S(1)} fusion(f32[128,64,8]{1,2,0:T(8,128)S(1)} %fusion.50, bf16[128,128,64]{0,2,1:T(8,128)(2,1)S(1)} %copy-done.3, f32[8,128,128]{1,0,2:T(8,128)S(1)} %copy-done.7), kind=kOutput, calls=%fused_computation.37 | convolution fusion | flops 100794368 | bytes 3014656 | tf_op jit(solution)/shard_map/tsq,sqr->tqr/dot_general | solution.py:69
  194.0 3.4 %fusion.25 = bf16[8,128,64]{2,0,1:T(8,128)(2,1)S(1)} fusion(f32[128,64,8]{1,2,0:T(8,128)S(1)} %fusion.51, bf16[128,128,64]{0,2,1:T(8,128)(2,1)S(1)} %copy.109, f32[8,128,128]{1,0,2:T(8,128)S(1)} %copy-done.7), kind=kOutput, calls=%fused_computation.36 | convolution fusion | flops 100794368 | bytes 3014656 | tf_op jit(solution)/shard_map/tsq,sqr->tqr/dot_general | solution.py:72
  197.4 0.2 pad_maximum_fusion.5
  197.5 0.7 copy.94
  198.3 7.8 %all-to-all-start.1 = ((bf16[8,128,128]{2,1,0:T(8,128)(2,1)}), bf16[8,128,128]{2,1,0:T(8,128)(2,1)S(1)}, u32[]{:S(2)}, u32[]{:S(2)}) async-start(bf16[8,128,128]{2,1,0:T(8,128)(2,1)} %copy.94), calls=%async_computation.1 | async-start | bytes 524288 | tf_op jit(solution)/shard_map/all_to_all | solution.py:136
  206.0 2.3 %slice_bitcast_fusion.2 = f32[16,128,128]{1,2,0:T(8,128)} fusion(f32[16,2,128,128]{2,3,1,0:T(8,128)} %fusion.15), kind=kLoop, calls=%fused_computation.38 | loop fusion | bytes 2097152 | tf_op jit(solution)/shard_map/squeeze | solution.py:115
  208.3 4.2 %all-to-all-done.1 = bf16[8,128,128]{2,1,0:T(8,128)(2,1)S(1)} async-done(((bf16[8,128,128]{2,1,0:T(8,128)(2,1)}), bf16[8,128,128]{2,1,0:T(8,128)(2,1)S(1)}, u32[]{:S(2)}, u32[]{:S(2)}) %all-to-all-start.1) | async-done | bytes 262176 | tf_op jit(solution)/shard_map/all_to_all | solution.py:136
  212.6 0.2 copy.95
  212.8 0.2 copy.97
  213.1 0.5 reshape.158
  213.6 0.5 reshape.159
  214.2 1.8 fusion.20
  216.0 0.3 slice_add_fusion
  216.3 1.3 copy-done.10
  217.5 0.2 fusion.29
  217.7 1.0 copy.98
  (61 shorter events, 1.2 us)
Async XLA Ops:
  0.0 119.3 %copy-start = (f32[316,2,1024]{2,1,0:T(2,128)S(1)}, f32[316,2,1024]{2,1,0:T(2,128)}, u32[]{:S(2)}) copy-start(f32[316,2,1024]{2,1,0:T(2,128)} %param.16) | copy-start | bytes 7766020
  3.7 5.8 %copy-start.2 = (f32[16,2,1024,128]{2,3,1,0:T(8,128)}, f32[16,2,1024,128]{2,3,1,0:T(8,128)S(1)}, u32[]{:S(2)}) copy-start(f32[16,2,1024,128]{2,3,1,0:T(8,128)S(1)} %convolution_bitcast_fusion) | copy-start | bytes 50331652
  31.0 5.1 %copy-start.16 = (f32[16,1024]{1,0:T(8,128)S(1)}, f32[16,1024]{1,0:T(8,128)}, u32[]{:S(2)}) copy-start(f32[16,1024]{1,0:T(8,128)} %param.15) | copy-start | bytes 196612
  31.0 5.4 %copy-start.4 = (f32[1,16,1024,64]{2,3,1,0:T(8,128)S(1)}, f32[1,16,1024,64]{2,3,1,0:T(8,128)}, u32[]{:S(2)}) copy-start(f32[1,16,1024,64]{2,3,1,0:T(8,128)} %get-tuple-element.12) | copy-start | bytes 12582916
  31.0 6.4 %copy-start.5 = (f32[1,16,1024,64]{2,3,1,0:T(8,128)S(1)}, f32[1,16,1024,64]{2,3,1,0:T(8,128)}, u32[]{:S(2)}) copy-start(f32[1,16,1024,64]{2,3,1,0:T(8,128)} %get-tuple-element.13) | copy-start | bytes 12582916
  36.4 8.8 %copy-start.12 = (f32[16,1024]{1,0:T(8,128)}, f32[16,1024]{1,0:T(8,128)S(1)}, u32[]{:S(2)}) copy-start(f32[16,1024]{1,0:T(8,128)S(1)} %get-tuple-element.27) | copy-start | bytes 196612
  36.4 8.8 %copy-start.14 = (f32[16,1024]{1,0:T(8,128)}, f32[16,1024]{1,0:T(8,128)S(1)}, u32[]{:S(2)}) copy-start(f32[16,1024]{1,0:T(8,128)S(1)} %get-tuple-element.28) | copy-start | bytes 196612
  60.6 28.7 %copy-start.6 = (bf16[16,128,128]{2,1,0:T(8,128)(2,1)S(1)}, bf16[16,128,128]{2,1,0:T(8,128)(2,1)}, u32[]{:S(2)}) copy-start(bf16[16,128,128]{2,1,0:T(8,128)(2,1)} %param.10) | copy-start | bytes 1572868
  61.6 35.8 %copy-start.17 = (s32[128,6]{0,1:T(8,128)S(1)}, s32[128,6]{0,1:T(8,128)}, u32[]{:S(2)}) copy-start(s32[128,6]{0,1:T(8,128)} %param.18) | copy-start | bytes 9220
  61.6 36.0 %copy-start.21 = (s32[128]{0:T(128)S(1)}, s32[128]{0:T(128)}, u32[]{:S(2)}) copy-start(s32[128]{0:T(128)} %param.19) | copy-start | bytes 1540
  62.7 6.9 %collective-permute-start.2 = (bf16[1,8,128,128]{3,2,1,0:T(8,128)(2,1)S(1)}, bf16[1,8,128,128]{3,2,1,0:T(8,128)(2,1)}, u32[]{:S(2)}, u32[]{:S(2)}) collective-permute-start(bf16[1,8,128,128]{3,2,1,0:T(8,128)(2,1)S(1)} %bitcast.125), channel_id=1, source_target_pairs={{0,8},{8,0},{16,24},{24,16},{32,40},{40,32},{48,56},{56,48},{64,72... | collective-permute-start | bytes 786440 | tf_op jit(solution)/shard_map/ppermute | solution.py:20
  71.9 13.3 %collective-permute-start.3 = (bf16[2,8,128,128]{3,2,1,0:T(8,128)(2,1)}, bf16[2,8,128,128]{3,2,1,0:T(8,128)(2,1)}, u32[]{:S(2)}, u32[]{:S(2)}) collective-permute-start(bf16[2,8,128,128]{3,2,1,0:T(8,128)(2,1)} %get-tuple-element.24), channel_id=1, source_target_pairs={{0,16},{8,24},{16,0},{24,8},{32,48},{40,56},{48,32},{56,40},{64,80... | collective-permute-start | bytes 1572872 | tf_op jit(solution)/shard_map/ppermute | solution.py:20
  87.7 24.3 %collective-permute-start.4 = (bf16[4,8,128,128]{3,2,1,0:T(8,128)(2,1)}, bf16[4,8,128,128]{3,2,1,0:T(8,128)(2,1)}, u32[]{:S(2)}, u32[]{:S(2)}) collective-permute-start(bf16[4,8,128,128]{3,2,1,0:T(8,128)(2,1)} %bitcast.25), channel_id=1, source_target_pairs={{0,32},{8,40},{16,48},{24,56},{32,0},{40,8},{48,16},{56,24},{64,96... | collective-permute-start | bytes 3145736 | tf_op jit(solution)/shard_map/ppermute | solution.py:20
  90.2 33.3 %collective-permute-start = (bf16[8,128,128]{2,1,0:T(8,128)(2,1)}, bf16[8,128,128]{2,1,0:T(8,128)(2,1)}, u32[]{:S(2)}, u32[]{:S(2)}) collective-permute-start(bf16[8,128,128]{2,1,0:T(8,128)(2,1)} %get-tuple-element.25), channel_id=1, source_target_pairs={{0,1},{1,2},{2,3},{3,4},{4,5},{5,6},{6,7},{7,8},{8,9},{9,10},{10,1... | collective-permute-start | bytes 786440 | tf_op jit(solution)/shard_map/ppermute | solution.py:35
  95.4 28.1 %collective-permute-start.1 = (bf16[8,128,128]{2,1,0:T(8,128)(2,1)}, bf16[8,128,128]{2,1,0:T(8,128)(2,1)}, u32[]{:S(2)}, u32[]{:S(2)}) collective-permute-start(bf16[8,128,128]{2,1,0:T(8,128)(2,1)} %get-tuple-element.26), channel_id=1, source_target_pairs={{1,0},{2,1},{3,2},{4,3},{5,4},{6,5},{7,6},{8,7},{9,8},{10,9},{11,1... | collective-permute-start | bytes 786440 | tf_op jit(solution)/shard_map/ppermute | solution.py:37
  112.0 7.0 %copy-start.18 = (s32[128,6]{0,1:T(8,128)S(1)}, s32[128,6]{0,1:T(8,128)}, u32[]{:S(2)}) copy-start(s32[128,6]{0,1:T(8,128)} %param.17) | copy-start | bytes 9220
  113.8 9.4 %copy-start.19 = (s32[16,8]{0,1:T(8,128)S(1)}, s32[16,8]{0,1:T(8,128)}, u32[]{:S(2)}) copy-start(s32[16,8]{0,1:T(8,128)} %param.12) | copy-start | bytes 1540
  113.8 9.4 %copy-start.20 = (s32[16]{0:T(128)S(1)}, s32[16]{0:T(128)}, u32[]{:S(2)}) copy-start(s32[16]{0:T(128)} %param.13) | copy-start | bytes 196
  115.7 45.8 %collective-permute-start.5 = (bf16[8,8,128,128]{3,2,1,0:T(8,128)(2,1)}, bf16[8,8,128,128]{3,2,1,0:T(8,128)(2,1)}, u32[]{:S(2)}, u32[]{:S(2)}) collective-permute-start(bf16[8,8,128,128]{3,2,1,0:T(8,128)(2,1)} %bitcast.28), channel_id=1, source_target_pairs={{0,64},{8,72},{16,80},{24,88},{32,96},{40,104},{48,112},{56,120},{... | collective-permute-start | bytes 6291464 | tf_op jit(solution)/shard_map/ppermute | solution.py:20
  175.7 6.6 %copy-start.8 = (f32[8,128,128]{1,0,2:T(8,128)S(1)}, f32[8,128,128]{1,0,2:T(8,128)}, u32[]{:S(2)}) copy-start(f32[8,128,128]{1,0,2:T(8,128)} %copy.89) | copy-start | bytes 1572868
  182.3 8.3 %copy-start.3 = (bf16[128,128,64]{0,2,1:T(8,128)(2,1)S(1)}, bf16[128,128,64]{0,2,1:T(8,128)(2,1)}, u32[]{:S(2)}) copy-start(bf16[128,128,64]{0,2,1:T(8,128)(2,1)} %copy.110) | copy-start | bytes 6291460
  182.3 8.3 %copy-start.7 = (f32[8,128,128]{1,0,2:T(8,128)S(1)}, f32[8,128,128]{1,0,2:T(8,128)}, u32[]{:S(2)}) copy-start(f32[8,128,128]{1,0,2:T(8,128)} %copy.91) | copy-start | bytes 1572868
  198.3 14.3 %all-to-all-start.1 = ((bf16[8,128,128]{2,1,0:T(8,128)(2,1)}), bf16[8,128,128]{2,1,0:T(8,128)(2,1)S(1)}, u32[]{:S(2)}, u32[]{:S(2)}) async-start(bf16[8,128,128]{2,1,0:T(8,128)(2,1)} %copy.94), calls=%async_computation.1 | async-start | bytes 524288 | tf_op jit(solution)/shard_map/all_to_all | solution.py:136
  213.0 1.1 copy-start.11
  213.0 1.1 copy-start.13
  213.0 1.1 copy-start.15
  214.1 1.8 copy-start.9
  214.1 4.6 %copy-start.1 = (f32[316,2,1024]{2,1,0:T(2,128)S(1)}, f32[316,2,1024]{2,1,0:T(2,128)}, u32[]{:S(2)}) copy-start(f32[316,2,1024]{2,1,0:T(2,128)} %param.16) | copy-start | bytes 7766020
  215.9 1.6 copy-start.10
